TPU v7x, 512 devices: a whole 4x8x8 slice. The times are simulated.
512 devices in a mesh: dp: 64 (over z, y), mp: 8 (over x, core).
Axes of the slice: x: 4, y: 8, z: 8, core: 2. Of those that a mesh axis runs over, the one named last changes fastest.
Arguments:
- spikes: bfloat16 [3584, 16, 384], P('dp'), may hold values from -6 to 6
- session_ids: int32 [3584, 1], P('dp'), may hold values from 0 to 63; in each aligned block of 56 rows (0 to 55, 56 to 111, ...) at most 2 rows name the same one
- readin: bfloat16 [64, 384, 4096], P('dp', None, 'mp')
- gain: float32 [4096], P('mp'), may hold values from 0.5 to 1.5
- proj: bfloat16 [4096, 2048], P('mp', 'dp'), may hold values from -0.09375 to 0.09375
- query_bias: float32 [2048], P('mp'), may hold values from -1.5 to 1.5
- cotangent: bfloat16 [3584, 16, 2048], P('dp', None, 'mp'), may hold values from -0.0234375 to 0.0234375
Outputs:
- readin_grad: float32 [64, 384, 4096], P('dp', None, 'mp')
- gain_grad: float32 [4096], P('mp')
- proj_grad: float32 [4096, 2048], P('mp', 'dp')
Inputs may be any that keep to these rules, and one draw needn't show every extreme that they name: `session_ids`: among the 56 windows of one device no session appears more than 2 times, and some session appears exactly 2 times.
All inputs are finite; a program needn't handle non-finite values.
Results may differ from a plain program's by a relative error of at most 0.011.
Values may be sent and summed in bfloat16 or wider, within the bound.
A program may use at most 64 MiB of HBM per device.

v0:
```python
import jax
import jax.numpy as jnp
from jax import lax
from jax.sharding import PartitionSpec as P

D = 4096
HD = 128
MOST = 2


eps_norm = 1e-05


def on_device(spikes, session_ids, readin, gain, proj, query_bias, cotangent):
    windows, bin_count, channels = spikes.shape
    owner_count = lax.axis_size("dp")
    slot_count = owner_count * MOST
    slice_width = readin.shape[2]
    row_count = windows * bin_count
    share = cotangent.shape[2]
    owners = session_ids[:, 0]
    positions = jnp.arange(windows)
    earlier = (owners[:, None] == owners[None, :]) & (positions[None, :] < positions[:, None])
    ranked = jnp.sum(earlier.astype(jnp.int32), axis=1)
    target = owners * MOST + ranked
    placing = (jnp.arange(slot_count)[:, None] == target[None, :]).astype(jnp.bfloat16)
    outgoing = jnp.dot(
        placing, spikes.reshape(windows, bin_count * channels), preferred_element_type=jnp.float32
    )
    outgoing = outgoing.astype(jnp.bfloat16).reshape(owner_count, MOST, bin_count, channels)
    table = readin[0]
    arrived = lax.all_to_all(outgoing, "dp", split_axis=0, concat_axis=0, tiled=True)
    items = arrived.shape[1]
    mapped = jnp.dot(arrived.reshape(-1, channels), table, preferred_element_type=jnp.float32)
    mapped = mapped.astype(jnp.bfloat16).reshape(owner_count, items, bin_count, slice_width)
    returned = lax.all_to_all(mapped, "dp", split_axis=0, concat_axis=0, tiled=True)
    returned, arrived = (returned, arrived)
    gathered_rows = lax.dot_general(
        placing,
        returned.reshape(slot_count, bin_count * slice_width),
        (((0,), (0,)), ((), ())),
        preferred_element_type=jnp.float32,
    )
    features = gathered_rows.reshape(row_count, slice_width)
    squares = lax.psum(jnp.sum(features * features, axis=-1), "mp")
    inverse = lax.rsqrt(squares / D + eps_norm)[:, None]
    normed = (features * inverse * gain).astype(jnp.bfloat16)
    whole_proj = lax.all_gather(proj, "dp", axis=1, tiled=True)
    partial_queries = jnp.dot(normed, whole_proj, preferred_element_type=jnp.float32)
    summed = lax.psum(partial_queries.astype(jnp.bfloat16), "mp").astype(jnp.float32)
    own_queries = lax.dynamic_slice_in_dim(summed, lax.axis_index("mp") * share, share, 1)
    own_queries = own_queries + query_bias
    queries = own_queries.reshape(row_count, share // HD, HD)
    scale = lax.rsqrt(jnp.mean(queries * queries, axis=-1, keepdims=True) + eps_norm)
    unit = queries * scale
    upstream = cotangent.reshape(row_count, share // HD, HD).astype(jnp.float32)
    own_grad = scale * (upstream - unit * jnp.mean(upstream * unit, axis=-1, keepdims=True))
    own_grad = own_grad.reshape(row_count, share).astype(jnp.bfloat16)
    query_grad = lax.all_gather(own_grad, "mp", axis=1, tiled=True)
    proj_grad = lax.psum_scatter(
        lax.dot_general(
            query_grad, normed, (((0,), (0,)), ((), ())), preferred_element_type=jnp.float32
        ),
        "dp",
        scatter_dimension=0,
        tiled=True,
    ).T
    normed_grad = lax.dot_general(
        query_grad, whole_proj, (((1,), (1,)), ((), ())), preferred_element_type=jnp.float32
    )
    scaled_grad = gain * normed_grad
    cross_sums = lax.psum(jnp.sum(scaled_grad * features, axis=-1), "mp")
    feature_grad = inverse * scaled_grad - features * inverse**3 * (cross_sums / D)[:, None]
    feature_grad = feature_grad.astype(jnp.bfloat16).reshape(windows, bin_count * slice_width)
    local_gain = jnp.sum(normed_grad * features * inverse, axis=0)
    gain_grad = lax.psum(local_gain, "dp")
    slotted = jnp.dot(placing, feature_grad, preferred_element_type=jnp.float32)
    slotted = slotted.astype(jnp.bfloat16).reshape(owner_count, MOST, bin_count, slice_width)
    incoming = lax.all_to_all(slotted, "dp", split_axis=0, concat_axis=0, tiled=True)
    readin_grad = lax.dot_general(
        arrived.reshape(-1, channels),
        incoming.reshape(-1, slice_width),
        (((0,), (0,)), ((), ())),
        preferred_element_type=jnp.float32,
    )
    return (readin_grad[None], gain_grad, proj_grad)


def solution(mesh):
    return jax.shard_map(
        on_device,
        mesh=mesh,
        in_specs=(
            P("dp", None, None),
            P("dp", None),
            P("dp", None, "mp"),
            P("mp"),
            P("mp", "dp"),
            P("mp"),
            P("dp", None, "mp"),
        ),
        out_specs=(P("dp", None, "mp"), P("mp"), P("mp", "dp")),
        check_vma=False,
    )
```

profile of v0, /device:TPU:4, one launch (start us, length us, event | category | flops | bytes accessed | tf_op | source)
XLA Modules:
  0.0 636.0 jit_solution(13360322924819784834)
XLA Ops:
  10.9 57.7 %all_to_all.15 = bf16[64,2,16,384]{3,2,1,0:T(8,128)(2,1)S(1)} all-to-all(bf16[64,2,16,384]{3,2,1,0:T(8,128)(2,1)S(1)} %bitcast.56), channel_id=1, replica_groups=mesh['dp'=64,'mp'=8] {'dp'}, dimensions={0} | all-to-all | bytes 3145728 | tf_op jit(solution)/shard_map/all_to_all | solution.py:32
  68.5 2.6 convolution_convert_fusion.3
  71.2 7.6 %all-to-all-start.1 = ((bf16[64,2,16,512]{3,2,1,0:T(8,128)(2,1)}), bf16[64,2,16,512]{3,2,1,0:T(8,128)(2,1)S(1)}, u32[]{:S(2)}, u32[]{:S(2)}) async-start(bf16[64,2,16,512]{3,2,1,0:T(8,128)(2,1)} %bitcast.60), calls=%async_computation.1 | async-start | bytes 4194304 | tf_op jit(solution)/shard_map/all_to_all | solution.py:36
  79.5 51.1 %all-to-all-done.1 = bf16[64,2,16,512]{3,2,1,0:T(8,128)(2,1)S(1)} async-done(((bf16[64,2,16,512]{3,2,1,0:T(8,128)(2,1)}), bf16[64,2,16,512]{3,2,1,0:T(8,128)(2,1)S(1)}, u32[]{:S(2)}, u32[]{:S(2)}) %all-to-all-start.1) | async-done | bytes 2097184 | tf_op jit(solution)/shard_map/all_to_all | solution.py:36
  132.0 1.7 fusion.4
  133.7 1.6 reshape.78
  135.6 10.7 %psum.28 = f32[896]{0:T(1024)S(1)} all-reduce(f32[896]{0:T(1024)S(1)} %multiply_reduce_fusion.2), channel_id=1, replica_groups=mesh['dp'=64,'mp'=8] {'mp'}, use_global_device_ids=true, to_apply=%region_2.0 | all-reduce | flops 896 | bytes 7168 | tf_op jit(solution)/shard_map/psum | solution.py:45
  146.3 38.7 %all-gather.3.cloned.1.call-done = bf16[512,2048]{0,1:T(8,128)(2,1)} async-done(((bf16[512,32]{0,1:T(8,128)(2,1)}), bf16[512,2048]{0,1:T(8,128)(2,1)}) %all-gather.3.cloned.1.call-update) | async-done | bytes 2097168 | tf_op jit(solution)/shard_map/all_gather | solution.py:48
  185.0 5.5 convolution_convert_fusion.2
  193.0 71.7 %all-reduce.2.cloned.1.call-done = bf16[896,2048]{1,0:T(8,128)(2,1)} async-done(((bf16[896,2048]{1,0:T(8,128)(2,1)}), bf16[896,2048]{1,0:T(8,128)(2,1)}) %all-reduce.2.cloned.1.call-update) | async-done | bytes 3670032 | tf_op jit(solution)/shard_map/psum | solution.py:50
  264.7 2.0 convert_add_fusion
  266.7 1.6 reshape.79
  269.5 12.7 %multiply_reduce_fusion.3 = f32[896,2]{1,0:T(8,128)S(1)} fusion(f32[896,2,128]{2,1,0:T(2,128)S(1)} %copy-done.1, f32[896,2,128]{2,1,0:T(2,128)S(1)} %reshape.79, f32[896,2]{1,0:T(8,128)S(1)} %add_rsqrt_fusion), kind=kLoop, calls=%fused_computation.15 | loop fusion | flops 686336 | bytes 1849344 | tf_op jit(solution)/shard_map/reduce_sum | solution.py:57
  284.4 2.1 fusion.2
  286.6 43.3 %all-gather.5.cloned.1.call-done = bf16[896,2048]{1,0:T(8,128)(2,1)} async-done(((bf16[896,256]{1,0:T(8,128)(2,1)}), bf16[896,2048]{1,0:T(8,128)(2,1)}) %all-gather.5.cloned.1.call-update) | async-done | bytes 3670032 | tf_op jit(solution)/shard_map/all_gather | solution.py:59
  329.9 6.4 %fusion.9 = f32[2048,512]{1,0:T(8,128)} fusion(bf16[896,2048]{1,0:T(8,128)(2,1)} %all-gather.5.cloned.1.call-done, f32[896,512]{1,0:T(8,128)S(1)} %reshape.78, f32[512]{0:T(512)S(1)} %copy-done.6, f32[896]{0:T(1024)S(1)} %get-tuple-element.6), kind=kOutput, calls=%fused_computation.33 | convolution fusion | flops 1880424448 | bytes 9704960 | tf_op jit(solution)/shard_map/dot_general | solution.py:61
  336.3 6.1 multiply_reduce_fusion
  342.5 10.5 %psum.30 = f32[896]{0:T(1024)S(1)} all-reduce(f32[896]{0:T(1024)S(1)} %get-tuple-element.4), channel_id=1, replica_groups=mesh['dp'=64,'mp'=8] {'mp'}, use_global_device_ids=true, to_apply=%region_7.0 | all-reduce | flops 896 | bytes 7168 | tf_op jit(solution)/shard_map/psum | solution.py:72
  353.0 1.9 subtract_convert_fusion
  356.1 2.2 copy.23
  358.2 13.3 %all-to-all-start.2 = ((bf16[64,2,16,512]{3,2,1,0:T(8,128)(2,1)}), bf16[64,2,16,512]{3,2,1,0:T(8,128)(2,1)S(1)}, u32[]{:S(2)}, u32[]{:S(2)}) async-start(bf16[64,2,16,512]{3,2,1,0:T(8,128)(2,1)} %bitcast.25), calls=%async_computation.2 | async-start | bytes 4194304 | tf_op jit(solution)/shard_map/all_to_all | solution.py:79
  371.5 183.1 %psum.31 = f32[512]{0:T(512)} all-reduce(f32[512]{0:T(512)S(1)} %get-tuple-element.3), channel_id=1, replica_groups=mesh['dp'=64,'mp'=8] {'dp'}, use_global_device_ids=true, to_apply=%region_9.0 | all-reduce | flops 512 | bytes 4096 | tf_op jit(solution)/shard_map/psum | solution.py:76
  554.6 3.3 convolution_bitcast_fusion
  557.9 71.6 %reduce-scatter.2.cloned.1.call-done = f32[32,512]{1,0:T(8,128)} async-done(((f32[2048,512]{1,0:T(8,128)}), f32[32,512]{1,0:T(8,128)}) %reduce-scatter.2.cloned.1.call-update) | async-done | bytes 65552 | tf_op jit(solution)/shard_map/reduce_scatter | solution.py:60
  (40 shorter events, 13.0 us)
Async XLA Ops:
  7.2 61.4 %copy-start = (bf16[1,384,512]{2,1,0:T(8,128)(2,1)S(1)}, bf16[1,384,512]{2,1,0:T(8,128)(2,1)}, u32[]{:S(2)}) copy-start(bf16[1,384,512]{2,1,0:T(8,128)(2,1)} %param.9) | copy-start | bytes 1179652
  68.5 2.6 copy-start.4
  71.2 59.5 %all-to-all-start.1 = ((bf16[64,2,16,512]{3,2,1,0:T(8,128)(2,1)}), bf16[64,2,16,512]{3,2,1,0:T(8,128)(2,1)S(1)}, u32[]{:S(2)}, u32[]{:S(2)}) async-start(bf16[64,2,16,512]{3,2,1,0:T(8,128)(2,1)} %bitcast.60), calls=%async_computation.1 | async-start | bytes 4194304 | tf_op jit(solution)/shard_map/all_to_all | solution.py:36
  78.8 106.2 %all-gather.3.cloned.1.call-start = ((), (), s32[]{:S(2)}) async-start(), calls=%async_computation.4 | async-start | bytes 2129920 | tf_op jit(solution)/shard_map/all_gather | solution.py:48
  79.5 185.2 %all-reduce.2.cloned.1.call-start = ((), (), s32[]{:S(2)}) async-start(), calls=%async_computation.5 | async-start | bytes 7340032 | tf_op jit(solution)/shard_map/psum | solution.py:50
  135.3 49.6 %copy-start.6 = (f32[512]{0:T(512)S(1)}, f32[512]{0:T(512)}, u32[]{:S(2)}) copy-start(f32[512]{0:T(512)} %param.10) | copy-start | bytes 6148
  190.5 1.0 copy-start.2
  190.5 74.1 %copy-start.5 = (f32[256]{0:T(256)S(1)}, f32[256]{0:T(256)}, u32[]{:S(2)}) copy-start(f32[256]{0:T(256)} %param.12) | copy-start | bytes 3076
  190.6 139.3 %all-gather.5.cloned.1.call-start = ((), (), s32[]{:S(2)}) async-start(), calls=%async_computation.6 | async-start | bytes 4128768 | tf_op jit(solution)/shard_map/all_gather | solution.py:59
  268.3 1.2 copy-start.1
  282.2 2.3 copy-start.3
  286.5 343.0 %reduce-scatter.2.cloned.1.call-start = ((), (), s32[]{:S(2)}) async-start(), calls=%async_computation.7 | async-start | bytes 4259840 | tf_op jit(solution)/shard_map/reduce_scatter | solution.py:60
  358.2 196.4 %all-to-all-start.2 = ((bf16[64,2,16,512]{3,2,1,0:T(8,128)(2,1)}), bf16[64,2,16,512]{3,2,1,0:T(8,128)(2,1)S(1)}, u32[]{:S(2)}, u32[]{:S(2)}) async-start(bf16[64,2,16,512]{3,2,1,0:T(8,128)(2,1)} %bitcast.25), calls=%async_computation.2 | async-start | bytes 4194304 | tf_op jit(solution)/shard_map/all_to_all | solution.py:79
Sparse Core Ops, SparseCore 0:
  82.7 102.2 all-gather.2
  190.7 73.9 all-reduce.1
  286.7 43.1 all-gather.4
  336.4 293.0 reduce-scatter.1
where the time goes:
time: 637 us; the launch traced here: 636 us
  waiting for transfers between devices  277 us (43%)
  blocking collectives  262 us (41%)
  matrix products  27 us (4%)
  other arithmetic  21.6 us (3%)
  starting transfers between devices  21.2 us (3%)
  between operations  13.9 us (2%)
  local copies, waits for them, and re-layouts  13.2 us (2%)
    psum x1, blocking collectives, on_device(): gain_grad = lax.psum(local_gain, 'dp')  183 us
    psum x1, waiting for transfers between devices, on_device(): lax.psum(partial_queries.astype(jnp.bfloat16), 'mp').astype(jnp.float32)  71.7 us
    reduce_scatter x1, waiting for transfers between devices, on_device(): lax.psum_scatter(lax.dot_general(query_grad, normed, (((0,), (0,)), ((),...  71.6 us
    all_to_all x1, blocking collectives, on_device(): lax.all_to_all(outgoing, 'dp', split_axis=0, concat_axis=0, tiled=True)  57.7 us
    all_to_all x1, waiting for transfers between devices, on_device(): lax.all_to_all(mapped, 'dp', split_axis=0, concat_axis=0, tiled=True)  51.1 us
    all_gather x1, waiting for transfers between devices, on_device(): query_grad = lax.all_gather(own_grad, 'mp', axis=1, tiled=True)  43.3 us
    all_gather x1, waiting for transfers between devices, on_device(): whole_proj = lax.all_gather(proj, 'dp', axis=1, tiled=True)  38.7 us
    all_to_all x1, starting transfers between devices, on_device(): lax.all_to_all(slotted, 'dp', split_axis=0, concat_axis=0, tiled=True)  13.3 us
  transfers between devices with their start and end apart: 6, of which 5 were waited for; matrix products, arithmetic and copies ran while one was open for 3% of the time, Pallas kernels for 0%

commit v1 on v0

v1 whole, which is shorter than its diff:
```python
import jax
import jax.numpy as jnp
from jax import lax
from jax.sharding import PartitionSpec as P

D = 4096
HD = 128
MOST = 2

eps_norm = 1e-05
F32 = jnp.float32
BF16 = jnp.bfloat16


def on_device(spikes, session_ids, readin, gain, proj, query_bias, cotangent):
    windows, bin_count, channels = spikes.shape
    owner_count = lax.axis_size("dp")
    mp_count = lax.axis_size("mp")
    slot_count = owner_count * MOST
    slice_width = readin.shape[2]
    share = cotangent.shape[2]
    owners = session_ids[:, 0]
    positions = jnp.arange(windows)
    earlier = (owners[:, None] == owners[None, :]) & (positions[None, :] < positions[:, None])
    ranked = jnp.sum(earlier.astype(jnp.int32), axis=1)
    target = owners * MOST + ranked
    placing = (jnp.arange(slot_count)[:, None] == target[None, :]).astype(BF16)

    def to_owner(rows):
        width = rows.shape[2]
        out = jnp.dot(placing, rows.reshape(windows, bin_count * width), preferred_element_type=F32)
        out = out.astype(BF16).reshape(owner_count, MOST * bin_count * width // 128, 128)
        out = lax.all_to_all(out, "dp", split_axis=0, concat_axis=0, tiled=True)
        return out.reshape(slot_count * bin_count, width)

    table = readin[0]
    scaled = (proj.astype(F32) * gain[:, None]).astype(BF16).T
    whole = lax.all_gather(scaled, "dp", axis=0, tiled=True)
    events = to_owner(spikes)
    upstream = to_owner(cotangent).astype(F32)
    maps = lax.dot_general(table, whole, (((1,), (1,)), ((), ())), preferred_element_type=F32)
    maps = maps.astype(BF16).reshape(channels, mp_count, share).transpose(1, 0, 2)
    maps = lax.all_to_all(maps, "mp", split_axis=0, concat_axis=0, tiled=True)
    maps = jnp.sum(maps.astype(F32), axis=0).astype(BF16)
    features = jnp.dot(events, table, preferred_element_type=F32)
    squares = lax.psum(jnp.sum(features * features, axis=-1), "mp")
    inverse = lax.rsqrt(squares / D + eps_norm)[:, None]
    raw = jnp.dot(events, maps, preferred_element_type=F32)
    tokens = raw.shape[0]
    queries = (raw * inverse + query_bias).reshape(tokens, share // HD, HD)
    scale = lax.rsqrt(jnp.mean(queries * queries, axis=-1, keepdims=True) + eps_norm)
    unit = queries * scale
    up = upstream.reshape(tokens, share // HD, HD)
    grad = scale * (up - unit * jnp.mean(up * unit, axis=-1, keepdims=True))
    grad = grad.reshape(tokens, share)
    cross = lax.psum(jnp.sum(grad * raw, axis=-1), "mp")
    weight = inverse**3 * (cross / D)[:, None]
    moved = (grad * inverse).astype(BF16)
    across = lax.dot_general(moved, events, (((0,), (0,)), ((), ())), preferred_element_type=F32)
    across = lax.all_gather(across.astype(BF16), "mp", axis=0, tiled=True)
    part = jnp.dot(across, table, preferred_element_type=F32).astype(BF16)
    part = part.reshape(owner_count, proj.shape[1], slice_width)
    part = lax.all_to_all(part, "dp", split_axis=0, concat_axis=0, tiled=True)
    total = jnp.sum(part.astype(F32), axis=0).T
    gain_grad = lax.psum(jnp.sum(total * proj.astype(F32), axis=1), "dp")
    proj_grad = total * gain[:, None]
    inner = lax.dot_general(
        events, (events.astype(F32) * weight).astype(BF16), (((0,), (0,)), ((), ())), preferred_element_type=F32
    )
    readin_grad = lax.dot_general(across, whole, (((0,), (0,)), ((), ())), preferred_element_type=F32)
    readin_grad = readin_grad - jnp.dot(inner.astype(BF16), table, preferred_element_type=F32)
    return (readin_grad[None], gain_grad, proj_grad)


def solution(mesh):
    return jax.shard_map(
        on_device,
        mesh=mesh,
        in_specs=(
            P("dp", None, None),
            P("dp", None),
            P("dp", None, "mp"),
            P("mp"),
            P("mp", "dp"),
            P("mp"),
            P("dp", None, "mp"),
        ),
        out_specs=(P("dp", None, "mp"), P("mp"), P("mp", "dp")),
        check_vma=False,
    )
```

time: 637 us -> 451 us (0.71)
  waiting for transfers between devices: 277 us -> 162 us
  blocking collectives: 262 us -> 170 us
  starting transfers between devices: 21.2 us -> 41.8 us
  local copies, waits for them, and re-layouts: 13.2 us -> 23.7 us
  other arithmetic: 21.6 us -> 15.1 us
    psum x1 -> x0, waiting for transfers between devices: 71.7 us -> none  [on_device(): lax.psum(partial_queries.astype(jnp.bfloat16), 'mp').astype(jnp.float32)]
    reduce_scatter x1 -> x0, waiting for transfers between devices: 71.6 us -> none  [on_device(): lax.psum_scatter(lax.dot_general(query_grad, normed, (((0,), (0,)), ((),...]
    all_to_all x1 -> x0, blocking collectives: 57.7 us -> none  [on_device(): lax.all_to_all(outgoing, 'dp', split_axis=0, concat_axis=0, tiled=True)]
    psum x2, blocking collectives: 194 us -> 152 us  [the longest x1 140 us: on_device(): gain_grad = lax.psum(jnp.sum(total * proj.astype(F32), axis=1), 'dp')]
    all_gather x2, waiting for transfers between devices: 82 us -> 105 us  [the longest x1 78.7 us: on_device(): whole = lax.all_gather(scaled, 'dp', axis=0, tiled=True)]
    all_to_all x2 -> x4, starting transfers between devices: 20.9 us -> 41.8 us  [the longest x2 23.1 us: to_owner(): out = lax.all_to_all(out, 'dp', split_axis=0, concat_axis=0, tiled=True)]
    psum x1, blocking collectives: 10.7 us -> 18.3 us  [on_device(): squares = lax.psum(jnp.sum(features * features, axis=-1), 'mp')]
    all_to_all x2 -> x4, waiting for transfers between devices: 51.1 us -> 56.9 us  [the longest x1 30.2 us: on_device(): part = lax.all_to_all(part, 'dp', split_axis=0, concat_axis=0, tiled=True)]
  transfers between devices with their start and end apart: 6 -> 6, of which waited for: 5 -> 4; matrix products, arithmetic and copies ran while one was open for 3% -> 6% of each run, Pallas kernels for 0% -> 0%
where the time goes in v1:
time: 451 us; the launch traced here: 450 us
  blocking collectives  170 us (38%)
  waiting for transfers between devices  162 us (36%)
  starting transfers between devices  41.8 us (9%)
  local copies, waits for them, and re-layouts  23.7 us (5%)
  matrix products  23.1 us (5%)
  other arithmetic  15.1 us (3%)
  between operations  14.3 us (3%)
    psum x1, blocking collectives, on_device(): gain_grad = lax.psum(jnp.sum(total * proj.astype(F32), axis=1), 'dp')  140 us
    all_gather x1, waiting for transfers between devices, on_device(): whole = lax.all_gather(scaled, 'dp', axis=0, tiled=True)  78.7 us
    all_to_all x1, waiting for transfers between devices, on_device(): part = lax.all_to_all(part, 'dp', split_axis=0, concat_axis=0, tiled=True)  30.2 us
    all_to_all x2, waiting for transfers between devices, to_owner(): out = lax.all_to_all(out, 'dp', split_axis=0, concat_axis=0, tiled=True)  26.7 us
    all_gather x1, waiting for transfers between devices, on_device(): across = lax.all_gather(across.astype(BF16), 'mp', axis=0, tiled=True)  26.1 us
    all_to_all x2, starting transfers between devices, to_owner(): out = lax.all_to_all(out, 'dp', split_axis=0, concat_axis=0, tiled=True)  23.1 us
    psum x1, blocking collectives, on_device(): squares = lax.psum(jnp.sum(features * features, axis=-1), 'mp')  18.3 us
    all_to_all x1, starting transfers between devices, on_device(): part = lax.all_to_all(part, 'dp', split_axis=0, concat_axis=0, tiled=True)  13.9 us
  transfers between devices with their start and end apart: 6, of which 4 were waited for; matrix products, arithmetic and copies ran while one was open for 6% of the time, Pallas kernels for 0%

profile of v1, /device:TPU:4, one launch (start us, length us, event | category | flops | bytes accessed | tf_op | source)
XLA Modules:
  0.0 449.6 jit_solution(1734245028871967589)
XLA Ops:
  11.7 16.7 %all-to-all-start.2 = ((bf16[64,64,128]{2,1,0:T(8,128)(2,1)}), bf16[64,64,128]{2,1,0:T(8,128)(2,1)S(1)}, u32[]{:S(2)}, u32[]{:S(2)}) async-start(bf16[64,64,128]{2,1,0:T(8,128)(2,1)} %reshape.93), calls=%async_computation.2 | async-start | bytes 2097152 | tf_op jit(solution)/shard_map/all_to_all | solution.py:33
  31.5 26.7 %all-to-all-done.2 = bf16[64,64,128]{2,1,0:T(8,128)(2,1)S(1)} async-done(((bf16[64,64,128]{2,1,0:T(8,128)(2,1)}), bf16[64,64,128]{2,1,0:T(8,128)(2,1)S(1)}, u32[]{:S(2)}, u32[]{:S(2)}) %all-to-all-start.2) | async-done | bytes 1048608 | tf_op jit(solution)/shard_map/all_to_all | solution.py:33
  58.3 6.4 %all-to-all-start = ((bf16[64,96,128]{2,1,0:T(8,128)(2,1)}), bf16[64,96,128]{2,1,0:T(8,128)(2,1)S(1)}, u32[]{:S(2)}, u32[]{:S(2)}) async-start(bf16[64,96,128]{2,1,0:T(8,128)(2,1)} %reshape.89), calls=%async_computation | async-start | bytes 3145728 | tf_op jit(solution)/shard_map/all_to_all | solution.py:33
  64.7 78.7 %all-gather.3.cloned.1.call-done = bf16[2048,512]{1,0:T(8,128)(2,1)} async-done(((bf16[32,512]{1,0:T(8,128)(2,1)}), bf16[2048,512]{1,0:T(8,128)(2,1)}) %all-gather.3.cloned.1.call-update) | async-done | bytes 2097168 | tf_op jit(solution)/shard_map/all_gather | solution.py:38
  143.3 4.0 convolution_convert_fusion.3
  147.3 4.8 %all-to-all-start.1 = ((bf16[8,384,256]{1,2,0:T(8,128)(2,1)}), bf16[8,384,256]{1,2,0:T(8,128)(2,1)}, u32[]{:S(2)}, u32[]{:S(2)}) async-start(bf16[8,384,256]{1,2,0:T(8,128)(2,1)} %bitcast.60), calls=%async_computation.1 | async-start | bytes 3145728 | tf_op jit(solution)/shard_map/all_to_all | solution.py:43
  153.6 2.9 copy.25
  158.6 18.3 %psum.21 = f32[2048]{0:T(1024)S(1)} all-reduce(f32[2048]{0:T(1024)S(1)} %multiply_reduce_fusion), channel_id=1, replica_groups=mesh['dp'=64,'mp'=8] {'mp'}, use_global_device_ids=true, to_apply=%region_3.0 | all-reduce | flops 2048 | bytes 16384 | tf_op jit(solution)/shard_map/psum | solution.py:46
  179.2 4.1 bitcast_reduce_fusion
  183.3 1.8 copy.22
  185.1 2.6 reshape.94
  190.0 2.5 rsqrt.17
  192.5 2.5 multiply_reduce_fusion.2
  195.6 1.8 div.17
  198.4 3.0 multiply_reduce_fusion.1
  202.9 26.1 %all-gather.5.cloned.1.call-done = bf16[2048,384]{1,0:T(8,128)(2,1)} async-done(((bf16[256,384]{1,0:T(8,128)(2,1)}), bf16[2048,384]{1,0:T(8,128)(2,1)}) %all-gather.5.cloned.1.call-update) | async-done | bytes 1572880 | tf_op jit(solution)/shard_map/all_gather | solution.py:60
  229.0 4.0 convolution_convert_fusion.2
  232.9 13.9 %all-to-all-start.3 = ((bf16[64,32,512]{2,1,0:T(8,128)(2,1)}), bf16[64,32,512]{2,1,0:T(8,128)(2,1)}, u32[]{:S(2)}, u32[]{:S(2)}) async-start(bf16[64,32,512]{2,1,0:T(8,128)(2,1)} %bitcast.58), calls=%async_computation.3 | async-start | bytes 4194304 | tf_op jit(solution)/shard_map/all_to_all | solution.py:63
  246.8 11.1 %psum.22 = f32[2048]{0:T(1024)S(1)} all-reduce(f32[2048]{0:T(1024)S(1)} %get-tuple-element.3), channel_id=1, replica_groups=mesh['dp'=64,'mp'=8] {'mp'}, use_global_device_ids=true, to_apply=%region_7.0 | all-reduce | flops 2048 | bytes 16384 | tf_op jit(solution)/shard_map/psum | solution.py:56
  262.2 4.1 fusion.15
  266.3 3.3 fusion.2
  269.6 30.2 %all-to-all-done.3 = bf16[64,32,512]{2,1,0:T(8,128)(2,1)} async-done(((bf16[64,32,512]{2,1,0:T(8,128)(2,1)}), bf16[64,32,512]{2,1,0:T(8,128)(2,1)}, u32[]{:S(2)}, u32[]{:S(2)}) %all-to-all-start.3) | async-done | bytes 2097184 | tf_op jit(solution)/shard_map/all_to_all | solution.py:63
  299.8 1.9 convert_reduce_fusion
  302.3 140.5 %psum.23 = f32[512]{0:T(512)} all-reduce(f32[512]{0:T(512)S(1)} %get-tuple-element.8), channel_id=1, replica_groups=mesh['dp'=64,'mp'=8] {'dp'}, use_global_device_ids=true, to_apply=%region_10.0 | all-reduce | flops 512 | bytes 4096 | tf_op jit(solution)/shard_map/psum | solution.py:65
  (72 shorter events, 23.5 us)
Async XLA Ops:
  7.2 136.1 %copy-start = (bf16[1,384,512]{2,1,0:T(8,128)(2,1)S(1)}, bf16[1,384,512]{2,1,0:T(8,128)(2,1)}, u32[]{:S(2)}) copy-start(bf16[1,384,512]{2,1,0:T(8,128)(2,1)} %param.9) | copy-start | bytes 1179652
  10.4 18.1 %copy-start.10 = (bf16[512,32]{0,1:T(8,128)(2,1)S(1)}, bf16[512,32]{0,1:T(8,128)(2,1)}, u32[]{:S(2)}) copy-start(bf16[512,32]{0,1:T(8,128)(2,1)} %param.11) | copy-start | bytes 98308
  10.4 18.1 %copy-start.16 = (f32[512]{0:T(512)S(1)}, f32[512]{0:T(512)}, u32[]{:S(2)}) copy-start(f32[512]{0:T(512)} %param.10) | copy-start | bytes 6148
  11.7 17.5 %copy-start.9 = (bf16[56,16,384]{2,1,0:T(8,128)(2,1)S(1)}, bf16[56,16,384]{2,1,0:T(8,128)(2,1)}, u32[]{:S(2)}) copy-start(bf16[56,16,384]{2,1,0:T(8,128)(2,1)} %param.7) | copy-start | bytes 2064388
  11.7 46.6 %all-to-all-start.2 = ((bf16[64,64,128]{2,1,0:T(8,128)(2,1)}), bf16[64,64,128]{2,1,0:T(8,128)(2,1)S(1)}, u32[]{:S(2)}, u32[]{:S(2)}) async-start(bf16[64,64,128]{2,1,0:T(8,128)(2,1)} %reshape.93), calls=%async_computation.2 | async-start | bytes 2097152 | tf_op jit(solution)/shard_map/all_to_all | solution.py:33
  28.4 114.9 %all-gather.3.cloned.1.call-start = ((), (), s32[]{:S(2)}) async-start(), calls=%async_computation.4 | async-start | bytes 2129920 | tf_op jit(solution)/shard_map/all_gather | solution.py:38
  58.3 93.9 %copy-start.6 = (bf16[64,64,128]{2,1,0:T(8,128)(2,1)}, bf16[64,64,128]{2,1,0:T(8,128)(2,1)S(1)}, u32[]{:S(2)}) copy-start(bf16[64,64,128]{2,1,0:T(8,128)(2,1)S(1)} %all-to-all-done.2) | copy-start | bytes 3145732
  58.3 89.1 %all-to-all-start = ((bf16[64,96,128]{2,1,0:T(8,128)(2,1)}), bf16[64,96,128]{2,1,0:T(8,128)(2,1)S(1)}, u32[]{:S(2)}, u32[]{:S(2)}) async-start(bf16[64,96,128]{2,1,0:T(8,128)(2,1)} %reshape.89), calls=%async_computation | async-start | bytes 3145728 | tf_op jit(solution)/shard_map/all_to_all | solution.py:33
  147.3 9.2 %copy-start.1 = (bf16[64,96,128]{2,1,0:T(8,128)(2,1)}, bf16[64,96,128]{2,1,0:T(8,128)(2,1)S(1)}, u32[]{:S(2)}) copy-start(bf16[64,96,128]{2,1,0:T(8,128)(2,1)S(1)} %all-to-all-done) | copy-start | bytes 4718596
  147.3 29.6 %all-to-all-start.1 = ((bf16[8,384,256]{1,2,0:T(8,128)(2,1)}), bf16[8,384,256]{1,2,0:T(8,128)(2,1)}, u32[]{:S(2)}, u32[]{:S(2)}) async-start(bf16[8,384,256]{1,2,0:T(8,128)(2,1)} %bitcast.60), calls=%async_computation.1 | async-start | bytes 3145728 | tf_op jit(solution)/shard_map/all_to_all | solution.py:43
  152.1 76.8 %all-gather.5.cloned.1.call-start = ((), (), s32[]{:S(2)}) async-start(), calls=%async_computation.5 | async-start | bytes 1769472 | tf_op jit(solution)/shard_map/all_gather | solution.py:60
  157.3 1.3 copy-start.3
  157.3 21.9 %copy-start.18 = (f32[256]{0:T(256)S(1)}, f32[256]{0:T(256)}, u32[]{:S(2)}) copy-start(f32[256]{0:T(256)} %param.12) | copy-start | bytes 3076
  176.9 6.3 %copy-start.12 = (f32[2048]{0:T(1024)}, f32[2048]{0:T(1024)S(1)}, u32[]{:S(2)}) copy-start(f32[2048]{0:T(1024)S(1)} %add_rsqrt_fusion.1) | copy-start | bytes 24580
  187.8 4.7 %copy-start.7 = (bf16[64,64,128]{2,1,0:T(8,128)(2,1)S(1)}, bf16[64,64,128]{2,1,0:T(8,128)(2,1)}, u32[]{:S(2)}) copy-start(bf16[64,64,128]{2,1,0:T(8,128)(2,1)} %copy-done.6) | copy-start | bytes 3145732
  198.4 3.0 copy-start.4
  198.4 3.0 copy-start.13
  232.9 24.9 %copy-start.15 = (f32[2048]{0:T(1024)S(1)}, f32[2048]{0:T(1024)}, u32[]{:S(2)}) copy-start(f32[2048]{0:T(1024)} %copy-done.14) | copy-start | bytes 24580
  232.9 25.9 %copy-start.2 = (bf16[64,96,128]{2,1,0:T(8,128)(2,1)S(1)}, bf16[64,96,128]{2,1,0:T(8,128)(2,1)}, u32[]{:S(2)}) copy-start(bf16[64,96,128]{2,1,0:T(8,128)(2,1)} %copy-done.1) | copy-start | bytes 4718596
  232.9 66.8 %all-to-all-start.3 = ((bf16[64,32,512]{2,1,0:T(8,128)(2,1)}), bf16[64,32,512]{2,1,0:T(8,128)(2,1)}, u32[]{:S(2)}, u32[]{:S(2)}) async-start(bf16[64,32,512]{2,1,0:T(8,128)(2,1)} %bitcast.58), calls=%async_computation.3 | async-start | bytes 4194304 | tf_op jit(solution)/shard_map/all_to_all | solution.py:63
  262.2 4.1 copy-start.5
  262.2 4.1 copy-start.8
  269.6 32.1 %copy-start.11 = (bf16[512,32]{0,1:T(8,128)(2,1)S(1)}, bf16[512,32]{0,1:T(8,128)(2,1)}, u32[]{:S(2)}) copy-start(bf16[512,32]{0,1:T(8,128)(2,1)} %param.11) | copy-start | bytes 98308
  269.6 32.1 %copy-start.17 = (f32[512]{0:T(512)S(1)}, f32[512]{0:T(512)}, u32[]{:S(2)}) copy-start(f32[512]{0:T(512)} %param.10) | copy-start | bytes 6148
  (1 other events, 0.6 us)
Sparse Core Ops, SparseCore 0:
  32.9 110.3 all-gather.2
  203.0 25.9 all-gather.4
